TPU v7x, 256 devices: a whole 4x4x8 slice. The times are simulated.
256 devices in a mesh: blk: 8 (over y, core), head: 8 (over z_hi, x), dp: 4 (over z_lo).
Axes of the slice: x: 4, y: 4, z: 8 (z_hi: 2, z_lo: 4; z = z_hi * 4 + z_lo), core: 2. Of those that a mesh axis runs over, the one named last changes fastest.
Arguments:
- queries: bfloat16 [16384, 2048], P(('dp', 'blk', 'head')), parts along dimension 0, may hold values from -10 to 10
- keys: bfloat16 [16384, 2048], P(('dp', 'blk', 'head')), parts along dimension 0, may hold values from -10 to 10
- values: bfloat16 [16384, 2048], P(('dp', 'blk', 'head')), parts along dimension 0, may hold values from -6 to 6
- outputs: bfloat16 [16384, 2048], P(('dp', 'blk', 'head')), parts along dimension 0, may hold values from -6 to 6
- d_outputs: bfloat16 [16384, 2048], P(('dp', 'blk', 'head')), parts along dimension 0, may hold values from -96 to 96
- tile_mask: int32 [32, 32], replicated, may hold values from 0 to 1, as said below
- tile_order: int32 [32], replicated, may hold values from 0 to 31, each once
Outputs:
- d_queries: bfloat16 [16384, 2048], P(('dp', 'blk', 'head')), parts along dimension 0
- d_keys: bfloat16 [16384, 2048], P(('dp', 'blk', 'head')), parts along dimension 0
- d_values: bfloat16 [16384, 2048], P(('dp', 'blk', 'head')), parts along dimension 0
There are 4 independent parts, one for each index of `dp`. A program takes and returns all parts, laid end to end along the dimension named above; an argument that names none is the same for every part. Nothing has to cross between parts.
Inputs may be any that keep to these rules, and one draw needn't show every extreme that they name: tile_mask[a, b] is 0 or 1, and 1 only where tile b lies in the window of min(3, n) tiles along each grid dimension of n tiles around tile a, shifted to stay inside; tiles are numbered with time slowest over a 2 x 4 x 4 grid; every diagonal entry is 1; in some row the whole window is 1.
All inputs are finite; a program needn't handle non-finite values.
Results may differ from a plain program's by a relative error of at most 0.005.
Values may be sent and summed in bfloat16 or wider, within the bound.
A program may use at most 64 MiB of HBM per device.

v0:
```python
import jax
import jax.numpy as jnp
from jax import lax
from jax.sharding import PartitionSpec as P

DH = 128
BLOCK = 128


key_span = 512
neg_large = -1e30


def tile_hot(tile_order, offset, row_count):
    tile_count = tile_order.shape[0]
    blocks = offset // BLOCK + jnp.arange(row_count // BLOCK, dtype=jnp.int32)
    columns = jnp.arange(tile_count, dtype=jnp.int32)
    tiles = jnp.sum(jnp.where(blocks[:, None] == columns[None, :], tile_order[None, :], 0), axis=1)
    return (tiles[:, None] == columns[None, :]).astype(jnp.float32)


def permitted(row_hot, col_hot, mask_float, row_count, col_count):
    linked = jnp.dot(jnp.dot(row_hot, mask_float), col_hot.T) > 0.5
    spread = jnp.broadcast_to(
        linked[:, None, :, None], (row_count // BLOCK, BLOCK, col_count // BLOCK, BLOCK)
    )
    return spread.reshape(row_count, col_count)[None]


def heads_view(source):
    return source.reshape(source.shape[0], -1, DH)


def attention_scores(query_rows, key_rows):
    factor = DH ** (-0.5)
    return (
        jnp.einsum(
            "qhd,khd->hqk",
            heads_view(query_rows),
            heads_view(key_rows),
            preferred_element_type=jnp.float32,
        )
        * factor
    )


def over_blocks(step_fn, carried, incoming):
    leaves = jax.tree.leaves(incoming)
    row_count = leaves[0].shape[0]
    block_count = row_count // key_span
    stacked = jax.tree.map(
        lambda source: source.reshape((block_count, key_span) + source.shape[1:]), incoming
    )

    def inner(running, item):
        block_index, block_rows = item
        return (step_fn(running, block_rows, block_index * key_span), None)

    carried, unused = lax.scan(inner, carried, (jnp.arange(block_count, dtype=jnp.int32), stacked))
    return carried


def block_scores(query_rows, dout_rows, lse_rows, delta_rows, key_rows, value_rows, allowed):
    factor = DH ** (-0.5)
    scores = attention_scores(query_rows, key_rows)
    probs = jnp.where(allowed, jnp.exp(scores - lse_rows[:, :, None]), 0.0)
    dprobs = jnp.einsum(
        "qhd,khd->hqk",
        heads_view(dout_rows),
        heads_view(value_rows),
        preferred_element_type=jnp.float32,
    )
    dscores = (factor * probs * (dprobs - delta_rows[:, :, None])).astype(jnp.bfloat16)
    return (dscores, probs.astype(jnp.bfloat16))


def query_term(dscores, key_rows, row_count):
    return jnp.einsum(
        "hqk,khd->qhd", dscores, heads_view(key_rows), preferred_element_type=jnp.float32
    ).reshape(row_count, -1)


def key_value_terms(dscores, probs_low, query_rows, dout_rows, row_count):
    key_part = jnp.einsum(
        "hqk,qhd->khd", dscores, heads_view(query_rows), preferred_element_type=jnp.float32
    )
    value_part = jnp.einsum(
        "hqk,qhd->khd", probs_low, heads_view(dout_rows), preferred_element_type=jnp.float32
    )
    return (key_part.reshape(row_count, -1), value_part.reshape(row_count, -1))


def block_grads(query_rows, dout_rows, lse_rows, delta_rows, key_rows, value_rows, allowed):
    dscores, probs_low = block_scores(
        query_rows, dout_rows, lse_rows, delta_rows, key_rows, value_rows, allowed
    )
    query_part = query_term(dscores, key_rows, query_rows.shape[0])
    key_part, value_part = key_value_terms(
        dscores, probs_low, query_rows, dout_rows, key_rows.shape[0]
    )
    return (query_part, key_part, value_part)


def body(queries, keys, values, outputs, d_outputs, tile_mask, tile_order):
    cycle_size = lax.axis_size("blk")
    cycle_rank = lax.axis_index("blk")
    query_loc, key_loc, value_loc, output_loc, dout_loc = (
        lax.all_to_all(queries, "head", split_axis=1, concat_axis=0, tiled=True),
        lax.all_to_all(keys, "head", split_axis=1, concat_axis=0, tiled=True),
        lax.all_to_all(values, "head", split_axis=1, concat_axis=0, tiled=True),
        lax.all_to_all(outputs, "head", split_axis=1, concat_axis=0, tiled=True),
        lax.all_to_all(d_outputs, "head", split_axis=1, concat_axis=0, tiled=True),
    )
    local_rows = query_loc.shape[0]
    all_rows = local_rows * cycle_size
    head_count = query_loc.shape[1] // DH
    feature_width = head_count * DH
    mask_float = tile_mask.astype(jnp.float32)
    own_hot = tile_hot(tile_order, cycle_rank * local_rows, local_rows)

    def first_block(carried, incoming, offset):
        row_top, row_total = carried
        row_count = incoming.shape[0]
        allowed = permitted(
            own_hot, tile_hot(tile_order, offset, row_count), mask_float, local_rows, row_count
        )
        masked = jnp.where(allowed, attention_scores(query_loc, incoming), neg_large)
        new_top = jnp.maximum(row_top, jnp.max(masked, axis=2))
        weights = jnp.where(allowed, jnp.exp(masked - new_top[:, :, None]), 0.0)
        return (new_top, row_total * jnp.exp(row_top - new_top) + jnp.sum(weights, axis=2))

    start_state = (
        jnp.full((head_count, local_rows), neg_large, jnp.float32),
        jnp.zeros((head_count, local_rows), jnp.float32),
    )
    row_top, row_total = over_blocks(
        first_block, start_state, lax.all_gather(key_loc, "blk", axis=0, tiled=True)
    )
    log_total = row_top + jnp.log(row_total)
    delta_all = jnp.sum(
        heads_view(dout_loc).astype(jnp.float32) * heads_view(output_loc).astype(jnp.float32),
        axis=2,
    ).T

    def second_block(carried, incoming, offset):
        query_grad, buffer = carried
        key_piece, value_piece = incoming
        row_count = key_piece.shape[0]
        allowed = permitted(
            own_hot, tile_hot(tile_order, offset, row_count), mask_float, local_rows, row_count
        )
        query_part, key_part, value_part = block_grads(
            query_loc, dout_loc, log_total, delta_all, key_piece, value_piece, allowed
        )
        update = jnp.concatenate([key_part, value_part], axis=1)
        current = lax.dynamic_slice_in_dim(buffer, offset, row_count, 0)
        buffer = lax.dynamic_update_slice_in_dim(buffer, current + update, offset, 0)
        return (query_grad + query_part, buffer)

    start_grads = (
        jnp.zeros((local_rows, feature_width), jnp.float32),
        jnp.zeros((all_rows, 2 * feature_width), jnp.float32),
    )
    query_grad, buffer = over_blocks(
        second_block,
        start_grads,
        (
            lax.all_gather(key_loc, "blk", axis=0, tiled=True),
            lax.all_gather(value_loc, "blk", axis=0, tiled=True),
        ),
    )
    own_part = lax.psum_scatter(buffer, "blk", scatter_dimension=0, tiled=True)
    key_grad = own_part[:, :feature_width]
    value_grad = own_part[:, feature_width:]
    return (
        lax.all_to_all(
            query_grad.astype(jnp.bfloat16), "head", split_axis=0, concat_axis=1, tiled=True
        ),
        lax.all_to_all(
            key_grad.astype(jnp.bfloat16), "head", split_axis=0, concat_axis=1, tiled=True
        ),
        lax.all_to_all(
            value_grad.astype(jnp.bfloat16), "head", split_axis=0, concat_axis=1, tiled=True
        ),
    )


def solution(mesh):
    in_specs = (
        P(("dp", "blk", "head"), None),
        P(("dp", "blk", "head"), None),
        P(("dp", "blk", "head"), None),
        P(("dp", "blk", "head"), None),
        P(("dp", "blk", "head"), None),
        P(),
        P(),
    )
    out_specs = (
        P(("dp", "blk", "head"), None),
        P(("dp", "blk", "head"), None),
        P(("dp", "blk", "head"), None),
    )
    return jax.shard_map(body, mesh=mesh, in_specs=in_specs, out_specs=out_specs, check_vma=False)
```

profile of v0, /device:TPU:1, one launch (start us, length us, event | category | flops | bytes accessed | tf_op | source)
XLA Modules:
  0.0 330.1 jit_solution(14974300982461669608)
XLA Ops:
  7.2 1.0 copy.184
  8.3 21.6 %all_to_all.146 = bf16[64,8,256]{2,0,1:T(8,128)(2,1)} all-to-all(bf16[64,8,256]{2,0,1:T(8,128)(2,1)S(1)} %bitcast.208), channel_id=1, replica_groups=mesh['blk'=8,'head'=8,'dp'=4] {'head'}, dimensions={1} | all-to-all | bytes 524288 | tf_op jit(solution)/shard_map/all_to_all | solution.py:109
  29.9 1.7 copy.183
  31.6 3.4 %all-to-all-start.1 = ((bf16[64,8,256]{2,0,1:T(8,128)(2,1)}), bf16[64,8,256]{2,0,1:T(8,128)(2,1)S(1)}, u32[]{:S(2)}, u32[]{:S(2)}) async-start(bf16[64,8,256]{2,0,1:T(8,128)(2,1)} %bitcast.116), calls=%async_computation.1 | async-start | bytes 524288 | tf_op jit(solution)/shard_map/all_to_all | solution.py:108
  35.7 9.2 %all-to-all-done.1 = bf16[64,8,256]{2,0,1:T(8,128)(2,1)S(1)} async-done(((bf16[64,8,256]{2,0,1:T(8,128)(2,1)}), bf16[64,8,256]{2,0,1:T(8,128)(2,1)S(1)}, u32[]{:S(2)}, u32[]{:S(2)}) %all-to-all-start.1) | async-done | bytes 262176 | tf_op jit(solution)/shard_map/all_to_all | solution.py:108
  44.9 3.4 %all-to-all-start.4 = ((bf16[64,8,256]{2,0,1:T(8,128)(2,1)}), bf16[64,8,256]{2,0,1:T(8,128)(2,1)S(1)}, u32[]{:S(2)}, u32[]{:S(2)}) async-start(bf16[64,8,256]{2,0,1:T(8,128)(2,1)} %bitcast.113), calls=%async_computation.4 | async-start | bytes 524288 | tf_op jit(solution)/shard_map/all_to_all | solution.py:111
  49.1 9.2 %all-to-all-done.4 = bf16[64,8,256]{2,0,1:T(8,128)(2,1)S(1)} async-done(((bf16[64,8,256]{2,0,1:T(8,128)(2,1)}), bf16[64,8,256]{2,0,1:T(8,128)(2,1)S(1)}, u32[]{:S(2)}, u32[]{:S(2)}) %all-to-all-start.4) | async-done | bytes 262176 | tf_op jit(solution)/shard_map/all_to_all | solution.py:111
  58.2 3.4 %all-to-all-start.3 = ((bf16[64,8,256]{2,0,1:T(8,128)(2,1)}), bf16[64,8,256]{2,0,1:T(8,128)(2,1)S(1)}, u32[]{:S(2)}, u32[]{:S(2)}) async-start(bf16[64,8,256]{2,0,1:T(8,128)(2,1)} %bitcast.114), calls=%async_computation.3 | async-start | bytes 524288 | tf_op jit(solution)/shard_map/all_to_all | solution.py:112
  62.6 9.1 %all-to-all-done.3 = bf16[64,8,256]{2,0,1:T(8,128)(2,1)S(1)} async-done(((bf16[64,8,256]{2,0,1:T(8,128)(2,1)}), bf16[64,8,256]{2,0,1:T(8,128)(2,1)S(1)}, u32[]{:S(2)}, u32[]{:S(2)}) %all-to-all-start.3) | async-done | bytes 262176 | tf_op jit(solution)/shard_map/all_to_all | solution.py:112
  71.7 3.4 %all-to-all-start.2 = ((bf16[64,8,256]{2,0,1:T(8,128)(2,1)}), bf16[64,8,256]{2,0,1:T(8,128)(2,1)S(1)}, u32[]{:S(2)}, u32[]{:S(2)}) async-start(bf16[64,8,256]{2,0,1:T(8,128)(2,1)} %bitcast.115), calls=%async_computation.2 | async-start | bytes 524288 | tf_op jit(solution)/shard_map/all_to_all | solution.py:110
  77.5 7.6 %all-to-all-done.2 = bf16[64,8,256]{2,0,1:T(8,128)(2,1)S(1)} async-done(((bf16[64,8,256]{2,0,1:T(8,128)(2,1)}), bf16[64,8,256]{2,0,1:T(8,128)(2,1)S(1)}, u32[]{:S(2)}, u32[]{:S(2)}) %all-to-all-start.2) | async-done | bytes 262176 | tf_op jit(solution)/shard_map/all_to_all | solution.py:110
  85.9 3.9 %copy.131 = bf16[8,512,256]{1,2,0:T(8,128)(2,1)} copy(bf16[8,512,256]{2,1,0:T(8,128)(2,1)} %bitcast.200) | data formatting | bytes 4194304
  89.8 34.1 %while.30 = (s32[]{:T(128)}, f32[2,512]{1,0:T(2,128)S(1)}, f32[2,512]{1,0:T(2,128)S(1)}, s32[8]{0:T(128)S(1)}, s32[32]{0:T(128)S(1)}, /*index=5*/bf16[4,32]{1,0:...) while((s32[]{:T(128)}, f32[2,512]{1,0:T(2,128)S(1)}, ...), condition=%wide.region_5.6_spmd.clone, body=%wide.region_1.5_spmd.clone.sunk | while | flops 138418720 | bytes 6607662 | solution.py:59
  91.8 1.0 constant_dynamic-slice_fusion.8
  96.1 1.0 constant_dynamic-slice_fusion.8
  100.4 1.0 constant_dynamic-slice_fusion.8
  104.6 1.0 constant_dynamic-slice_fusion.8
  108.9 1.0 constant_dynamic-slice_fusion.8
  113.2 1.0 constant_dynamic-slice_fusion.8
  117.4 1.0 constant_dynamic-slice_fusion.8
  121.7 1.0 constant_dynamic-slice_fusion.8
  124.0 4.3 %broadcast_in_dim.140.clone = f32[4096,512]{1,0:T(8,128)} broadcast(f32[]{:T(128)} %constant.160.clone.1), dimensions={} | broadcast | bytes 8388612 | tf_op jit(solution)/shard_map/broadcast_in_dim | solution.py:162
  128.3 102.0 %while.31 = (s32[]{:T(128)}, f32[512,256]{0,1:T(8,128)S(1)}, f32[4096,512]{1,0:T(8,128)}, bf16[8,512,256]{1,2,0:T(8,128)(2,1)}, s32[8]{0:T(128)S(1)}, /*index=5*...) while((s32[]{:T(128)}, f32[512,256]{0,1:T(8,128)S(1)}, ...), condition=%wide.region_9.10_spmd.clone, body=%wide.region_7.9_spmd.clone.sunk | while | flops 676070912 | bytes 28582776 | solution.py:59
  132.1 1.0 constant_dynamic-slice_fusion.9
  133.1 1.3 constant_dynamic-slice_fusion.11
  134.7 1.8 bitcast_select_fusion.3
  137.8 1.4 fusion.77
  140.0 1.0 constant_dynamic-update-slice_fusion.2
  145.8 1.3 constant_dynamic-slice_fusion.11
  147.5 1.8 bitcast_select_fusion.3
  150.5 1.4 fusion.77
  152.7 1.1 constant_dynamic-update-slice_fusion.2
  158.6 1.3 constant_dynamic-slice_fusion.11
  160.2 1.8 bitcast_select_fusion.3
  163.3 1.4 fusion.77
  165.5 1.1 constant_dynamic-update-slice_fusion.2
  171.3 1.3 constant_dynamic-slice_fusion.11
  173.0 1.8 bitcast_select_fusion.3
  176.1 1.4 fusion.77
  178.2 1.1 constant_dynamic-update-slice_fusion.2
  183.1 1.0 constant_dynamic-slice_fusion.9
  184.1 1.3 constant_dynamic-slice_fusion.11
  185.7 1.8 bitcast_select_fusion.3
  188.8 1.4 fusion.77
  191.0 1.0 constant_dynamic-update-slice_fusion.2
  196.8 1.3 constant_dynamic-slice_fusion.11
  198.4 1.8 bitcast_select_fusion.3
  201.5 1.4 fusion.77
  203.7 1.1 constant_dynamic-update-slice_fusion.2
  209.5 1.3 constant_dynamic-slice_fusion.11
  211.2 1.8 bitcast_select_fusion.3
  214.3 1.4 fusion.77
  216.4 1.1 constant_dynamic-update-slice_fusion.2
  221.3 1.0 constant_dynamic-slice_fusion.9
  222.3 1.3 constant_dynamic-slice_fusion.11
  223.9 1.8 bitcast_select_fusion.3
  227.0 1.4 fusion.77
  229.2 1.1 constant_dynamic-update-slice_fusion.2
  231.1 3.4 %all-to-all-start.5 = ((bf16[8,64,256]{2,1,0:T(8,128)(2,1)}), bf16[8,64,256]{2,1,0:T(8,128)(2,1)S(1)}, u32[]{:S(2)}, u32[]{:S(2)}) async-start(bf16[8,64,256]{2,1,0:T(8,128)(2,1)} %bitcast.13), calls=%async_computation.5 | async-start | bytes 524288 | tf_op jit(solution)/shard_map/all_to_all | solution.py:176
  234.6 54.0 %reduce-scatter.2.cloned.1.call-done = f32[512,512]{1,0:T(8,128)} async-done(((f32[4096,512]{1,0:T(8,128)}), f32[512,512]{1,0:T(8,128)}) %reduce-scatter.2.cloned.1.call-update) | async-done | bytes 1048592 | tf_op jit(solution)/shard_map/reduce_scatter | solution.py:172
  288.6 1.3 convert.5
  290.6 18.9 %all_to_all.147 = bf16[8,64,256]{2,1,0:T(8,128)(2,1)S(1)} all-to-all(bf16[8,64,256]{2,1,0:T(8,128)(2,1)S(1)} %bitcast.209), channel_id=1, replica_groups=mesh['blk'=8,'head'=8,'dp'=4] {'head'}, dimensions={0} | all-to-all | bytes 524288 | tf_op jit(solution)/shard_map/all_to_all | solution.py:179
  309.5 3.4 %all-to-all-start.7 = ((bf16[8,64,256]{2,1,0:T(8,128)(2,1)}), bf16[8,64,256]{2,1,0:T(8,128)(2,1)S(1)}, u32[]{:S(2)}, u32[]{:S(2)}) async-start(bf16[8,64,256]{2,1,0:T(8,128)(2,1)} %bitcast.17), calls=%async_computation.8 | async-start | bytes 524288 | tf_op jit(solution)/shard_map/all_to_all | solution.py:182
  314.4 8.5 %all-to-all-done.7 = bf16[8,64,256]{2,1,0:T(8,128)(2,1)S(1)} async-done(((bf16[8,64,256]{2,1,0:T(8,128)(2,1)}), bf16[8,64,256]{2,1,0:T(8,128)(2,1)S(1)}, u32[]{:S(2)}, u32[]{:S(2)}) %all-to-all-start.7) | async-done | bytes 262176 | tf_op jit(solution)/shard_map/all_to_all | solution.py:182
  (257 shorter events, 78.0 us)
Async XLA Ops:
  7.2 27.8 %copy-start.1 = (bf16[64,2048]{1,0:T(8,128)(2,1)S(1)}, bf16[64,2048]{1,0:T(8,128)(2,1)}, u32[]{:S(2)}) copy-start(bf16[64,2048]{1,0:T(8,128)(2,1)} %param.14) | copy-start | bytes 786436
  7.2 41.1 %copy-start.2 = (bf16[64,2048]{1,0:T(8,128)(2,1)S(1)}, bf16[64,2048]{1,0:T(8,128)(2,1)}, u32[]{:S(2)}) copy-start(bf16[64,2048]{1,0:T(8,128)(2,1)} %param.15) | copy-start | bytes 786436
  7.2 78.7 %all-gather.3.cloned.1.call-start = ((), (), s32[]{:S(2)}) async-start(), calls=%async_computation.9 | async-start | bytes 2359296 | tf_op jit(solution)/shard_map/all_gather | solution.py:168
  8.2 53.5 %copy-start.3 = (bf16[64,2048]{1,0:T(8,128)(2,1)S(1)}, bf16[64,2048]{1,0:T(8,128)(2,1)}, u32[]{:S(2)}) copy-start(bf16[64,2048]{1,0:T(8,128)(2,1)} %param.13) | copy-start | bytes 786436
  29.9 32.6 %copy-start.5 = (s32[32]{0:T(128)S(1)}, s32[32]{0:T(128)}, u32[]{:S(2)}) copy-start(s32[32]{0:T(128)} %param.17) | copy-start | bytes 388
  29.9 45.3 %copy-start.4 = (s32[32,32]{1,0:T(8,128)S(1)}, s32[32,32]{1,0:T(8,128)}, u32[]{:S(2)}) copy-start(s32[32,32]{1,0:T(8,128)} %param.16) | copy-start | bytes 12292
  31.6 13.3 %all-to-all-start.1 = ((bf16[64,8,256]{2,0,1:T(8,128)(2,1)}), bf16[64,8,256]{2,0,1:T(8,128)(2,1)S(1)}, u32[]{:S(2)}, u32[]{:S(2)}) async-start(bf16[64,8,256]{2,0,1:T(8,128)(2,1)} %bitcast.116), calls=%async_computation.1 | async-start | bytes 524288 | tf_op jit(solution)/shard_map/all_to_all | solution.py:108
  44.9 13.3 %all-to-all-start.4 = ((bf16[64,8,256]{2,0,1:T(8,128)(2,1)}), bf16[64,8,256]{2,0,1:T(8,128)(2,1)S(1)}, u32[]{:S(2)}, u32[]{:S(2)}) async-start(bf16[64,8,256]{2,0,1:T(8,128)(2,1)} %bitcast.113), calls=%async_computation.4 | async-start | bytes 524288 | tf_op jit(solution)/shard_map/all_to_all | solution.py:111
  58.2 13.5 %all-to-all-start.3 = ((bf16[64,8,256]{2,0,1:T(8,128)(2,1)}), bf16[64,8,256]{2,0,1:T(8,128)(2,1)S(1)}, u32[]{:S(2)}, u32[]{:S(2)}) async-start(bf16[64,8,256]{2,0,1:T(8,128)(2,1)} %bitcast.114), calls=%async_computation.3 | async-start | bytes 524288 | tf_op jit(solution)/shard_map/all_to_all | solution.py:112
  71.7 13.3 %all-to-all-start.2 = ((bf16[64,8,256]{2,0,1:T(8,128)(2,1)}), bf16[64,8,256]{2,0,1:T(8,128)(2,1)S(1)}, u32[]{:S(2)}, u32[]{:S(2)}) async-start(bf16[64,8,256]{2,0,1:T(8,128)(2,1)} %bitcast.115), calls=%async_computation.2 | async-start | bytes 524288 | tf_op jit(solution)/shard_map/all_to_all | solution.py:110
  75.2 48.8 %all-gather.5.cloned.1.call-start = ((), (), s32[]{:S(2)}) async-start(), calls=%async_computation.10 | async-start | bytes 2359296 | tf_op jit(solution)/shard_map/all_gather | solution.py:169
  85.1 0.7 copy-start
  85.8 202.8 %reduce-scatter.2.cloned.1.call-start = ((), (), s32[]{:S(2)}) async-start(), calls=%async_computation.11 | async-start | bytes 9437184 | tf_op jit(solution)/shard_map/reduce_scatter | solution.py:172
  231.1 59.5 %all-to-all-start.5 = ((bf16[8,64,256]{2,1,0:T(8,128)(2,1)}), bf16[8,64,256]{2,1,0:T(8,128)(2,1)S(1)}, u32[]{:S(2)}, u32[]{:S(2)}) async-start(bf16[8,64,256]{2,1,0:T(8,128)(2,1)} %bitcast.13), calls=%async_computation.5 | async-start | bytes 524288 | tf_op jit(solution)/shard_map/all_to_all | solution.py:176
  309.5 13.3 %all-to-all-start.7 = ((bf16[8,64,256]{2,1,0:T(8,128)(2,1)}), bf16[8,64,256]{2,1,0:T(8,128)(2,1)S(1)}, u32[]{:S(2)}, u32[]{:S(2)}) async-start(bf16[8,64,256]{2,1,0:T(8,128)(2,1)} %bitcast.17), calls=%async_computation.8 | async-start | bytes 524288 | tf_op jit(solution)/shard_map/all_to_all | solution.py:182
Sparse Core Ops, SparseCore 0:
  30.0 27.4 all-gather.2
  85.9 31.9 all-gather.4
  230.4 58.0 reduce-scatter.1
where the time goes:
time: 336 us; the launch traced here: 330 us
  waiting for transfers between devices  97.7 us (29%)
  local copies, waits for them, and re-layouts  88.3 us (26%)
  matrix products  44.2 us (13%)
  blocking collectives  40.5 us (12%)
  starting transfers between devices  20.6 us (6%)
  between operations  14 us (4%)
  other arithmetic  12.8 us (4%)
  loops' own time  12 us (4%)
    reduce_scatter x1, waiting for transfers between devices, body(): own_part = lax.psum_scatter(buffer, 'blk', scatter_dimension=0, tiled=True)  54 us
    dynamic_slice x48, local copies, waits for them, and re-layouts, over_blocks(): lax.scan(inner, carried, (jnp.arange(block_count, dtype=jnp.int32), stack...  34 us
    all_to_all x1, blocking collectives, body(): lax.all_to_all(keys, 'head', split_axis=1, concat_axis=0, tiled=True)  21.6 us
    dot_general x16, matrix products, attention_scores(): jnp.einsum('qhd,khd->hqk', heads_view(query_rows), heads_view(key_rows),...  19.4 us
    all_to_all x1, blocking collectives, body(): lax.all_to_all(key_grad.astype(jnp.bfloat16), 'head', split_axis=0, conca...  18.9 us
    dynamic_slice x16, local copies, waits for them, and re-layouts, second_block(): current = lax.dynamic_slice_in_dim(buffer, offset, row_count, 0)  13.1 us
    another operation x2, loops' own time, over_blocks(): lax.scan(inner, carried, (jnp.arange(block_count, dtype=jnp.int32), stack...  12 us
    dot_general x8, matrix products, key_value_terms(): jnp.einsum('hqk,qhd->khd', dscores, heads_view(query_rows), preferred_ele...  11.4 us
  transfers between devices with their start and end apart: 9, of which 6 were waited for; matrix products, arithmetic and copies ran while one was open for 13% of the time, Pallas kernels for 0%

commit v1 on v0

v1 whole, which is shorter than its diff:
```python
import jax
import jax.numpy as jnp
from jax import lax
from jax.experimental import pallas as pl
from jax.experimental.pallas import tpu as pltpu
from jax.sharding import PartitionSpec as P

DH = 128
BLOCK = 128
ROWS = 64
CHIPS = 16
GROUP = 4 * ROWS
HALF = CHIPS * ROWS
CHUNK = 256
SCALE = DH**-0.5
LOG2E = 1.4426950408889634
MESH = pl.DeviceIdType.MESH
BF16 = jnp.bfloat16
F32 = jnp.float32

NT = (((1,), (1,)), ((), ()))
NN = (((1,), (0,)), ((), ()))
TN = (((0,), (0,)), ((), ()))


def mm(a, b, dims):
    return lax.dot_general(a, b, dims, preferred_element_type=F32)


def rows(start, size):
    return pl.ds(pl.multiple_of(start, size), size)


def kernel(
    q_ref, k_ref, v_ref, o_ref, g_ref, mask_ref, order_ref,
    dq_ref, dk_ref, dv_ref,
    qb, kb, vb, gb, ee, dka, dva, rka, rva, dqa, dqs, dqr, oq, ok, ov,
    dcol, dsrc, drec, stm, str_, bias,
    s_in, r_in, s_z, r_z, s_c, r_c, s_d, r_d, s_st, r_st, s_dz, r_dz, s_kv, r_kv, s_out, r_out,
):
    blk = lax.axis_index("blk")
    hd = lax.axis_index("head")
    dp = lax.axis_index("dp")
    y, c = blk // 2, blk % 2
    g, x = hd // 4, hd % 4
    me = y * 4 + x

    def plane(px, py):
        return (py * 2 + c, g * 4 + px, dp)

    across = (blk, (1 - g) * 4 + x, dp)
    sibling = (y * 2 + 1 - c, hd, dp)

    def remote(src, dst, ss, rs, to):
        return pltpu.make_async_remote_copy(
            src_ref=src, dst_ref=dst, send_sem=ss, recv_sem=rs, device_id=to, device_id_type=MESH
        )

    def took(ref, sem):
        pltpu.make_async_copy(ref, ref, sem).wait()

    def peer(k):
        px, py = (x + k % 4) % 4, (y + k // 4) % 4
        return px, py, py * 4 + px

    barrier = pltpu.get_barrier_semaphore()

    def greet(k, carry):
        px, py, unused = peer(k)
        pl.semaphore_signal(barrier, inc=1, device_id=plane(px, py), device_id_type=MESH)
        return carry

    pl.semaphore_signal(barrier, inc=1, device_id=across, device_id_type=MESH)
    lax.fori_loop(1, CHIPS, greet, 0)
    pl.semaphore_signal(barrier, inc=1, device_id=sibling, device_id_type=MESH)

    dcol[...] = jnp.zeros_like(dcol)
    prod = g_ref[...].astype(F32) * o_ref[...].astype(F32)
    lane = lax.broadcasted_iota(jnp.int32, (ROWS, BLOCK), 1)
    cols = jnp.zeros((ROWS, BLOCK), F32)
    for h in range(CHIPS):
        part = jnp.sum(prod[:, h * DH : (h + 1) * DH], axis=1, keepdims=True)
        cols = jnp.where(lane == h, part, cols)
    dcol[rows((x % 2) * ROWS, ROWS), :] = cols
    turned = dcol[...].T
    for h in range(CHIPS):
        dsrc[h] = turned[h : h + 1, :]

    pl.semaphore_wait(barrier, 17)

    sources = (q_ref, k_ref, g_ref, v_ref)
    targets = (qb.at[0], kb.at[c], gb.at[0], vb.at[c])
    mine = rows(me * ROWS, ROWS)
    for a in range(4):
        here = sources[a].at[:, rows(me * DH, DH)]
        pltpu.make_async_copy(here, targets[a].at[mine], r_in.at[a, y]).start()

        def send(k, carry):
            px, py, who = peer(k)
            remote(
                sources[a].at[:, rows(who * DH, DH)], targets[a].at[mine], s_in.at[a], r_in.at[a, y], plane(px, py)
            ).start()
            return carry

        lax.fori_loop(1, CHIPS, send, 0)
        if a == 1:
            pltpu.make_async_copy(dsrc.at[me], drec.at[me], r_d).start()

            def send_delta(k, carry):
                px, py, who = peer(k)
                remote(dsrc.at[who], drec.at[me], s_d, r_d, plane(px, py)).start()
                return carry

            lax.fori_loop(1, CHIPS, send_delta, 0)

    def block_of(j, core, half):
        return ((j // 2) * 2 + core) * 4 + half * 2 + j % 2

    def bias_row(i, carry):
        key_tile = order_ref[block_of(i % 8, i // 8, g)]
        for half in range(2):
            for j in range(8):
                query_tile = order_ref[block_of(j, c, g if half == 0 else 1 - g)]
                allowed = mask_ref[query_tile, key_tile]
                value = jnp.where(allowed == 1, 0.0, -1.0e30).astype(F32)
                bias[half, i, :, j * BLOCK : (j + 1) * BLOCK] = jnp.full((1, BLOCK), value, F32)
        return carry

    lax.fori_loop(0, 16, bias_row, 0)

    dka[...] = jnp.zeros_like(dka)
    dva[...] = jnp.zeros_like(dva)

    def group(k):
        return (y + 4 - k) % 4

    def forward_z(a, buf):
        def one(k, carry):
            yy = group(k)
            part = rows(yy * GROUP, GROUP)
            took(buf.at[0, part], r_in.at[2 * a, yy])
            remote(buf.at[0, part], buf.at[1, part], s_z.at[a], r_z.at[a, yy], across).start()
            return carry

        lax.fori_loop(0, 4, one, 0)

    def forward_core(a, buf):
        def one(k, carry):
            yy = group(k)
            part = rows(yy * GROUP, GROUP)
            took(buf.at[c, part], r_in.at[2 * a + 1, yy])
            remote(buf.at[c, part], buf.at[c, part], s_c.at[a], r_c.at[a], sibling).start()
            return carry

        lax.fori_loop(0, 4, one, 0)

    chunks = 2 * HALF // CHUNK

    def key_part(i):
        return i // (HALF // CHUNK), rows(i % (HALF // CHUNK) * CHUNK, CHUNK)

    def weigh(half, yy):
        lanes = rows(yy * GROUP, GROUP)
        query = qb[half, lanes, :]

        def first(i, top):
            core, part = key_part(i)
            s = mm(kb[core, part, :], query, NT) * (SCALE * LOG2E)
            low = s[:BLOCK] + bias[half, 2 * i, :, lanes]
            high = s[BLOCK:] + bias[half, 2 * i + 1, :, lanes]
            ee[half, yy, pl.ds(pl.multiple_of(i * CHUNK, CHUNK), BLOCK), :] = low
            ee[half, yy, pl.ds(pl.multiple_of(i * CHUNK + BLOCK, BLOCK), BLOCK), :] = high
            both = jnp.maximum(low, high).reshape(BLOCK // 8, 8, GROUP)
            return jnp.maximum(top, jnp.max(both, axis=0))

        top = lax.fori_loop(0, chunks, first, jnp.full((8, GROUP), -3.0e38, F32))
        top = jnp.max(top, axis=0, keepdims=True)

        def second(i, total):
            part = rows(i * CHUNK, CHUNK)
            e = jnp.exp2(ee[half, yy, part, :] - top)
            ee[half, yy, part, :] = e
            return total + jnp.sum(e.reshape(CHUNK // 8, 8, GROUP), axis=0)

        total = lax.fori_loop(0, chunks, second, jnp.zeros((8, GROUP), F32))
        stm[3 * half : 3 * half + 1, lanes] = top
        stm[3 * half + 1 : 3 * half + 2, lanes] = jnp.sum(total, axis=0, keepdims=True)

    def gradients(half, yy):
        lanes = rows(yy * GROUP, GROUP)
        query = qb[half, lanes, :]
        dout = gb[half, lanes, :]
        there = 3 - 3 * half
        top, total = stm[3 * half : 3 * half + 1, lanes], stm[3 * half + 1 : 3 * half + 2, lanes]
        top_r, total_r = str_[there : there + 1, lanes], str_[there + 1 : there + 2, lanes]
        high = jnp.maximum(top, top_r)
        ours = jnp.exp2(top - high)
        factor = ours / (total * ours + total_r * jnp.exp2(top_r - high))
        delta = stm[2:3, lanes] if half == 0 else str_[2:3, lanes]

        def one(i, dq):
            core, part = key_part(i)
            dprobs = mm(vb[core, part, :], dout, NT)
            probs = ee[half, yy, rows(i * CHUNK, CHUNK), :] * factor
            ds = (probs * (dprobs - delta)).astype(BF16)
            dva[core, part, :] += mm(probs.astype(BF16), dout, NN)
            dka[core, part, :] += mm(ds, query, NN)
            return dq + mm(ds, kb[core, part, :], TN)

        return lax.fori_loop(0, chunks, one, jnp.zeros((GROUP, DH), F32)) * SCALE

    forward_z(0, qb)
    forward_core(0, kb)
    took(kb.at[1 - c], r_c.at[0])

    def weigh_own(k, carry):
        weigh(0, group(k))
        return carry

    lax.fori_loop(0, 4, weigh_own, 0)
    forward_z(1, gb)
    forward_core(1, vb)

    took(drec, r_d)
    for j in range(8):
        stm[2:3, j * BLOCK : (j + 1) * BLOCK] = drec[2 * j] + drec[2 * j + 1]

    def weigh_other(k, carry):
        yy = group(k)
        took(qb.at[1, rows(yy * GROUP, GROUP)], r_z.at[0, yy])
        weigh(1, yy)
        return carry

    lax.fori_loop(0, 4, weigh_other, 0)
    swap = remote(stm, str_, s_st, r_st, across)
    swap.start()
    took(vb.at[1 - c], r_c.at[1])
    swap.wait_recv()

    def own(k, carry):
        yy = group(k)
        dqa[rows(yy * GROUP, GROUP), :] = gradients(0, yy)
        return carry

    lax.fori_loop(0, 4, own, 0)

    def other(k, carry):
        yy = group(k)
        part = rows(yy * GROUP, GROUP)
        took(gb.at[1, part], r_z.at[1, yy])
        dqs[part, :] = gradients(1, yy).astype(BF16)
        remote(dqs.at[part], dqr.at[part], s_dz, r_dz.at[yy], across).start()
        return carry

    lax.fori_loop(0, 4, other, 0)

    remote(dka.at[1 - c], rka, s_kv.at[0], r_kv.at[0], sibling).start()
    remote(dva.at[1 - c], rva, s_kv.at[1], r_kv.at[1], sibling).start()

    def give(buf, out, a):
        pltpu.make_async_copy(buf.at[mine], out.at[:, rows(me * DH, DH)], r_out.at[a]).start()

        def send(k, carry):
            px, py, who = peer(k)
            remote(
                buf.at[rows(who * ROWS, ROWS)], out.at[:, rows(me * DH, DH)], s_out.at[a], r_out.at[a], plane(px, py)
            ).start()
            return carry

        lax.fori_loop(1, CHIPS, send, 0)

    took(rka, r_kv.at[0])
    ok[...] = ((dka[c] + rka[...]) * SCALE).astype(BF16)
    give(ok, dk_ref, 1)
    took(rva, r_kv.at[1])
    ov[...] = (dva[c] + rva[...]).astype(BF16)
    give(ov, dv_ref, 2)

    for k in range(4):
        yy = group(k)
        part = rows(yy * GROUP, GROUP)
        took(dqr.at[part], r_dz.at[yy])
        oq[part, :] = (dqa[part, :] + dqr[part, :].astype(F32)).astype(BF16)
        for kx in range(4):
            px = (x + kx) % 4
            piece = oq.at[rows((yy * 4 + px) * ROWS, ROWS)]
            out = dq_ref.at[:, rows(me * DH, DH)]
            if k == 0 and kx == 0:
                pltpu.make_async_copy(piece, out, r_out.at[0]).start()
            else:
                remote(piece, out, s_out.at[0], r_out.at[0], plane(px, yy)).start()

    sent = pl.ds(0, HALF - ROWS)
    for a in range(4):
        took(qb.at[0, sent], s_in.at[a])
    took(drec.at[pl.ds(0, CHIPS - 1)], s_d)
    for a in range(2):
        took(qb.at[0], s_z.at[a])
        took(qb.at[0], s_c.at[a])
        took(rka, s_kv.at[a])
    swap.wait_send()
    took(dqs, s_dz)
    for a, out in enumerate((dq_ref, dk_ref, dv_ref)):
        took(out, r_out.at[a])
        took(qb.at[0, sent], s_out.at[a])


def body(queries, keys, values, outputs, d_outputs, tile_mask, tile_order):
    half = (HALF, DH)
    dma = pltpu.SemaphoreType.DMA
    vmem = pl.BlockSpec(memory_space=pltpu.VMEM)
    smem = pl.BlockSpec(memory_space=pltpu.SMEM)
    return pl.pallas_call(
        kernel,
        out_shape=[jax.ShapeDtypeStruct(queries.shape, BF16)] * 3,
        in_specs=[vmem] * 5 + [smem] * 2,
        out_specs=[vmem] * 3,
        scratch_shapes=[
            pltpu.VMEM((2,) + half, BF16),
            pltpu.VMEM((2,) + half, BF16),
            pltpu.VMEM((2,) + half, BF16),
            pltpu.VMEM((2,) + half, BF16),
            pltpu.VMEM((2, 4, 2 * HALF, GROUP), F32),
            pltpu.VMEM((2,) + half, F32),
            pltpu.VMEM((2,) + half, F32),
            pltpu.VMEM(half, F32),
            pltpu.VMEM(half, F32),
            pltpu.VMEM(half, F32),
            pltpu.VMEM(half, BF16),
            pltpu.VMEM(half, BF16),
            pltpu.VMEM(half, BF16),
            pltpu.VMEM(half, BF16),
            pltpu.VMEM(half, BF16),
            pltpu.VMEM((BLOCK, BLOCK), F32),
            pltpu.VMEM((CHIPS, 1, BLOCK), F32),
            pltpu.VMEM((CHIPS, 1, BLOCK), F32),
            pltpu.VMEM((8, HALF), F32),
            pltpu.VMEM((8, HALF), F32),
            pltpu.VMEM((2, 16, 1, HALF), F32),
            dma((4,)), dma((4, 4)),
            dma((2,)), dma((2, 4)),
            dma((2,)), dma((2,)),
            dma, dma,
            dma, dma,
            dma, dma((4,)),
            dma((2,)), dma((2,)),
            dma((3,)), dma((3,)),
        ],
        compiler_params=pltpu.CompilerParams(
            collective_id=0, has_side_effects=True, vmem_limit_bytes=48 * 2**20
        ),
        cost_estimate=pl.CostEstimate(flops=5 * 2**30, bytes_accessed=2**21, transcendentals=2**22),
        name="attention_backward",
    )(queries, keys, values, outputs, d_outputs, tile_mask, tile_order)


def solution(mesh):
    split = P(("dp", "blk", "head"), None)
    return jax.shard_map(
        body,
        mesh=mesh,
        in_specs=(split,) * 5 + (P(), P()),
        out_specs=(split,) * 3,
        check_vma=False,
    )
```

time: 336 us -> 98.6 us (0.29); the launches traced: 330 us -> 98.3 us
  waiting for transfers between devices: 97.7 us -> 0 us
  Pallas kernels: 0 us -> 89.4 us
  local copies, waits for them, and re-layouts: 88.3 us -> 8.22 us
  matrix products: 44.2 us -> 0 us
  blocking collectives: 40.5 us -> 0 us
  starting transfers between devices: 20.6 us -> 0 us
  between operations: 14 us -> 0.66 us
  other arithmetic: 12.8 us -> 0 us
  loops' own time: 12 us -> 0 us
    pallas_call x0 -> x1, Pallas kernels: none -> 89.4 us  [body(): pl.pallas_call(kernel, out_shape=[jax.ShapeDtypeStruct(queries.shape, BF1...]
    reduce_scatter x1 -> x0, waiting for transfers between devices: 54 us -> none  [body(): own_part = lax.psum_scatter(buffer, 'blk', scatter_dimension=0, tiled=True)]
    dynamic_slice x64 -> x0, local copies, waits for them, and re-layouts: 47.1 us -> none  [the longest x48 34 us: over_blocks(): lax.scan(inner, carried, (jnp.arange(block_count, dtype=jnp.int32), stack...]
    dot_general x65 -> x0, matrix products: 44.2 us -> none  [the longest x16 19.4 us: attention_scores(): jnp.einsum('qhd,khd->hqk', heads_view(query_rows), heads_view(key_rows),...]
    all_to_all x6 -> x0, waiting for transfers between devices: 43.6 us -> none  [the longest x1 9.18 us: body(): lax.all_to_all(outputs, 'head', split_axis=1, concat_axis=0, tiled=True)]
    all_to_all x2 -> x0, blocking collectives: 40.5 us -> none  [the longest x1 21.6 us: body(): lax.all_to_all(keys, 'head', split_axis=1, concat_axis=0, tiled=True)]
    all_to_all x6 -> x0, starting transfers between devices: 20.5 us -> none  [the longest x1 3.41 us: body(): lax.all_to_all(outputs, 'head', split_axis=1, concat_axis=0, tiled=True)]
    another operation x2 -> x0, loops' own time: 12 us -> none  [over_blocks(): lax.scan(inner, carried, (jnp.arange(block_count, dtype=jnp.int32), stack...]
  transfers between devices with their start and end apart: 9 -> 0, of which waited for: 6 -> 0; matrix products, arithmetic and copies ran while one was open for 13% -> 0% of each run, Pallas kernels for 0% -> 0%
where the time goes in v1:
time: 98.6 us; the launch traced here: 98.3 us
  Pallas kernels  89.4 us (91%)
  local copies, waits for them, and re-layouts  8.22 us (8%)
    pallas_call x1, Pallas kernels, body(): pl.pallas_call(kernel, out_shape=[jax.ShapeDtypeStruct(queries.shape, BF1...  89.4 us
    unnamed x17, local copies, waits for them, and re-layouts  8.22 us

profile of v1, /device:TPU:1, one launch (start us, length us, event | category | flops | bytes accessed | tf_op | source)
XLA Modules:
  0.0 98.3 jit_solution(12439060654507863805)
XLA Ops:
  0.6 0.0 copy-start
  0.6 0.9 copy-done
  1.6 0.0 copy-start.1
  1.6 0.9 copy-done.1
  2.5 0.0 copy-start.2
  2.5 0.9 copy-done.2
  3.5 0.0 copy-start.3
  3.5 0.9 copy-done.3
  4.4 0.0 copy-start.4
  4.4 0.9 copy-done.4
  5.4 0.0 copy-start.5
  5.4 0.7 copy-done.5
  6.1 0.0 copy-start.6
  6.1 0.7 copy-done.6
  6.8 89.4 %attention_backward.1 = (bf16[64,2048]{1,0:T(8,128)(2,1)S(1)}, bf16[64,2048]{1,0:T(8,128)(2,1)S(1)}, bf16[64,2048]{1,0:T(8,128)(2,1)S(1)}) custom-call(bf16[64,2048]{1,0:T(8,128)(2,1)S(1)} %copy-done, bf16[64,2048]{1,0:T(8,128)(2,1)S(1)} %copy-done.1, bf16[64,2048]{1,0:T(8,128)(2,1)S(1)} %copy-done.2, bf16[64,2048]{1,0:T(8,128)(2,1)S(1)} %copy-done.3, ...), custom_call_target="tpu_custom_call" | custom-call | flops 5368709120 | bytes 2097152 | tf_op jit(solution)/shard_map/attention_backward/pallas_call | solution.py:313
  96.2 0.7 copy.13
  96.9 0.7 copy.14
  97.6 0.7 copy.15
Async XLA Ops:
  0.6 1.0 copy-start
  1.6 0.9 copy-start.1
  2.5 0.9 copy-start.2
  3.5 0.9 copy-start.3
  4.4 0.9 copy-start.4
  5.4 0.7 copy-start.5
  6.1 0.7 copy-start.6

commit v2 on v1

v2 whole, which is shorter than its diff:
```python
import jax
import jax.numpy as jnp
from jax import lax
from jax.experimental import pallas as pl
from jax.experimental.pallas import tpu as pltpu
from jax.sharding import PartitionSpec as P

DH = 128
BLOCK = 128
ROWS = 64
CHIPS = 16
GROUP = 4 * ROWS
HALF = CHIPS * ROWS
SCALE = DH**-0.5
LOG2E = 1.4426950408889634
MESH = pl.DeviceIdType.MESH
BF16 = jnp.bfloat16
F32 = jnp.float32

NT = (((1,), (1,)), ((), ()))
NN = (((1,), (0,)), ((), ()))
TN = (((0,), (0,)), ((), ()))


def mm(a, b, dims):
    return lax.dot_general(a, b, dims, preferred_element_type=F32)


def rows(start, size):
    return pl.ds(pl.multiple_of(start, size), size)


def kernel(
    q_ref, k_ref, v_ref, o_ref, g_ref, mask_hbm, order_hbm,
    dq_ref, dk_ref, dv_ref,
    qb, kb, vb, gb, ee, dka, dva, rka, rva, dqa, dqs, dqr, oq, ok, ov,
    ol, gl, mask_ref, order_ref, dcol, dsrc, drec, st_own, st_oth, pr_own, pr_oth, bias,
    s_ld, s_in, r_in, s_z, r_z, s_c, r_c, s_d, r_d, s_st, r_st, s_so, r_so, s_dz, r_dz, s_kv, r_kv, s_out, r_out,
):
    blk = lax.axis_index("blk")
    hd = lax.axis_index("head")
    dp = lax.axis_index("dp")
    y, c = blk // 2, blk % 2
    g, x = hd // 4, hd % 4
    me = y * 4 + x

    def plane(px, py):
        return (py * 2 + c, g * 4 + px, dp)

    across = (blk, (1 - g) * 4 + x, dp)
    sibling = (y * 2 + 1 - c, hd, dp)

    def remote(src, dst, ss, rs, to):
        return pltpu.make_async_remote_copy(
            src_ref=src, dst_ref=dst, send_sem=ss, recv_sem=rs, device_id=to, device_id_type=MESH
        )

    def took(ref, sem):
        pltpu.make_async_copy(ref, ref, sem).wait()

    def peer(k):
        px, py = (x + k % 4) % 4, (y + k // 4) % 4
        return px, py, py * 4 + px

    barrier = pltpu.get_barrier_semaphore()

    def greet(k, carry):
        px, py, unused = peer(k)
        pl.semaphore_signal(barrier, inc=1, device_id=plane(px, py), device_id_type=MESH)
        return carry

    pl.semaphore_signal(barrier, inc=1, device_id=across, device_id_type=MESH)
    lax.fori_loop(1, CHIPS, greet, 0)
    pl.semaphore_signal(barrier, inc=1, device_id=sibling, device_id_type=MESH)

    loads = [
        pltpu.make_async_copy(src, dst, s_ld.at[n])
        for n, (src, dst) in enumerate(((o_ref, ol), (g_ref, gl), (mask_hbm, mask_ref), (order_hbm, order_ref)))
    ]
    for load in loads:
        load.start()
    pl.semaphore_wait(barrier, 17)

    sources = (q_ref, k_ref, g_ref, v_ref)
    mine = rows(me * ROWS, ROWS)
    mine_kv = rows(c * HALF + me * ROWS, ROWS)
    targets = (qb.at[0, mine], kb.at[mine_kv], gb.at[0, mine], vb.at[mine_kv])
    for a in range(4):
        here = sources[a].at[:, rows(me * DH, DH)]
        pltpu.make_async_copy(here, targets[a], r_in.at[a, y]).start()

        def send(k, carry):
            px, py, who = peer(k)
            remote(
                sources[a].at[:, rows(who * DH, DH)], targets[a], s_in.at[a], r_in.at[a, y], plane(px, py)
            ).start()
            return carry

        lax.fori_loop(1, CHIPS, send, 0)

    def group(k):
        return (y + 4 - k) % 4

    def forward_z(a, buf, first, last):
        def one(k, carry):
            yy = group(k)
            part = rows(yy * GROUP, GROUP)
            took(buf.at[0, part], r_in.at[2 * a, yy])
            remote(buf.at[0, part], buf.at[1, part], s_z.at[a], r_z.at[a, yy], across).start()
            return carry

        lax.fori_loop(first, last, one, 0)

    def forward_core(a, buf):
        def one(k, carry):
            yy = group(k)
            part = rows(c * HALF + yy * GROUP, GROUP)
            took(buf.at[part], r_in.at[2 * a + 1, yy])
            remote(buf.at[part], buf.at[part], s_c.at[a], r_c.at[a], sibling).start()
            return carry

        lax.fori_loop(0, 4, one, 0)

    forward_z(0, qb, 0, 4)

    for load in loads:
        load.wait()

    dcol[...] = jnp.zeros_like(dcol)
    prod = gl[...].astype(F32) * ol[...].astype(F32)
    lane = lax.broadcasted_iota(jnp.int32, (ROWS, BLOCK), 1)
    cols = jnp.zeros((ROWS, BLOCK), F32)
    for h in range(CHIPS):
        part = jnp.sum(prod[:, h * DH : (h + 1) * DH], axis=1, keepdims=True)
        cols = jnp.where(lane == h, part, cols)
    dcol[rows((x % 2) * ROWS, ROWS), :] = cols
    turned = dcol[...].T
    for h in range(CHIPS):
        dsrc[h] = turned[h : h + 1, :]

    pltpu.make_async_copy(dsrc.at[me], drec.at[me], r_d).start()

    def send_delta(k, carry):
        px, py, who = peer(k)
        remote(dsrc.at[who], drec.at[me], s_d, r_d, plane(px, py)).start()
        return carry

    lax.fori_loop(1, CHIPS, send_delta, 0)

    def block_of(j, core, half):
        return ((j // 2) * 2 + core) * 4 + half * 2 + j % 2

    def bias_row(i, carry):
        key_tile = order_ref[block_of(i % 8, i // 8, g)]
        for half in range(2):
            for j in range(8):
                query_tile = order_ref[block_of(j, c, g if half == 0 else 1 - g)]
                allowed = mask_ref[query_tile, key_tile]
                value = jnp.where(allowed == 1, 0.0, -1.0e30).astype(F32)
                bias[half, i, :, j * BLOCK : (j + 1) * BLOCK] = jnp.full((1, BLOCK), value, F32)
        return carry

    lax.fori_loop(0, 16, bias_row, 0)
    dka[...] = jnp.zeros_like(dka)
    dva[...] = jnp.zeros_like(dva)

    def weigh(half, yy, stats):
        lanes = rows(yy * GROUP, GROUP)
        s = mm(kb[...], qb[half, lanes, :], NT) * (SCALE * LOG2E)
        top = jnp.full((8, GROUP), -3.0e38, F32)
        for i in range(16):
            part = s[i * BLOCK : (i + 1) * BLOCK] + bias[half, i, :, lanes]
            ee[half, yy, i * BLOCK : (i + 1) * BLOCK, :] = part
            top = jnp.maximum(top, jnp.max(part.reshape(BLOCK // 8, 8, GROUP), axis=0))
        top = jnp.max(top, axis=0, keepdims=True)
        e = jnp.exp2(ee[half, yy] - top)
        ee[half, yy] = e
        total = jnp.sum(e.reshape(2 * HALF // 8, 8, GROUP), axis=0)
        stats[yy, 0] = top
        stats[yy, 1] = jnp.sum(total, axis=0, keepdims=True)

    def gradients(half, yy, stats, theirs, delta):
        lanes = rows(yy * GROUP, GROUP)
        query = qb[half, lanes, :]
        dout = gb[half, lanes, :]
        top, total, top_r, total_r = stats[yy, 0], stats[yy, 1], theirs[yy, 0], theirs[yy, 1]
        high = jnp.maximum(top, top_r)
        ours = jnp.exp2(top - high)
        factor = ours / (total * ours + total_r * jnp.exp2(top_r - high))
        e = ee[half, yy]
        ds = (e * (factor * SCALE) * (mm(vb[...], dout, NT) - delta)).astype(BF16)
        dva[...] += mm((e * factor).astype(BF16), dout, NN)
        dka[...] += mm(ds, query, NN)
        return mm(ds, kb[...], TN)

    def weigh_own(k, carry):
        weigh(0, group(k), st_own)
        return carry

    def weigh_other(k, carry):
        yy = group(k)
        took(qb.at[1, rows(yy * GROUP, GROUP)], r_z.at[0, yy])
        weigh(1, yy, st_oth)
        remote(st_oth.at[yy], pr_oth.at[yy], s_so, r_so.at[yy], across).start()
        return carry

    def own(k, carry):
        yy = group(k)
        took(pr_oth.at[yy], r_so.at[yy])
        dqa[rows(yy * GROUP, GROUP), :] = gradients(0, yy, st_own, pr_oth, st_own[yy, 2])
        return carry

    def other(k, carry):
        yy = group(k)
        part = rows(yy * GROUP, GROUP)
        took(gb.at[1, part], r_z.at[1, yy])
        dqs[part, :] = gradients(1, yy, st_oth, pr_own, pr_own[yy, 2]).astype(BF16)
        remote(dqs.at[part], dqr.at[part], s_dz, r_dz.at[yy], across).start()
        return carry

    forward_core(0, kb)
    forward_z(1, gb, 0, 1)
    took(kb.at[pl.ds((1 - c) * HALF, HALF)], r_c.at[0])
    lax.fori_loop(0, 3, weigh_other, 0)
    forward_z(1, gb, 1, 2)
    forward_core(1, vb)
    lax.fori_loop(0, 4, weigh_own, 0)
    took(drec, r_d)
    for j in range(8):
        st_own[j // 2, 2, :, j % 2 * BLOCK : (j % 2 + 1) * BLOCK] = drec[2 * j] + drec[2 * j + 1]
    tell = remote(st_own, pr_own, s_st, r_st, across)
    tell.start()
    lax.fori_loop(3, 4, weigh_other, 0)
    forward_z(1, gb, 2, 4)
    took(vb.at[pl.ds((1 - c) * HALF, HALF)], r_c.at[1])
    lax.fori_loop(0, 3, own, 0)
    tell.wait_recv()
    lax.fori_loop(0, 2, other, 0)
    lax.fori_loop(3, 4, own, 0)
    lax.fori_loop(2, 4, other, 0)

    for k in range(4):
        yy = group(k)
        part = rows(yy * GROUP, GROUP)
        there = rows((1 - c) * HALF + yy * GROUP, GROUP)
        remote(dva.at[there], rva.at[part], s_kv.at[1], r_kv.at[1, yy], sibling).start()
        remote(dka.at[there], rka.at[part], s_kv.at[0], r_kv.at[0, yy], sibling).start()

    def give(k, buf, out, a):
        yy = group(k)
        for kx in range(4):
            px = (x + kx) % 4
            piece = buf.at[rows((yy * 4 + px) * ROWS, ROWS)]
            home = out.at[:, rows(me * DH, DH)]
            if k == 0 and kx == 0:
                pltpu.make_async_copy(piece, home, r_out.at[a]).start()
            else:
                remote(piece, home, s_out.at[a], r_out.at[a], plane(px, yy)).start()

    for k in range(4):
        yy = group(k)
        part = rows(yy * GROUP, GROUP)
        here = rows(c * HALF + yy * GROUP, GROUP)
        took(rva.at[part], r_kv.at[1, yy])
        ov[part, :] = (dva[here, :] + rva[part, :]).astype(BF16)
        give(k, ov, dv_ref, 2)
        took(rka.at[part], r_kv.at[0, yy])
        ok[part, :] = (dka[here, :] + rka[part, :]).astype(BF16)
        give(k, ok, dk_ref, 1)
    for k in range(4):
        yy = group(k)
        part = rows(yy * GROUP, GROUP)
        took(dqr.at[part], r_dz.at[yy])
        oq[part, :] = (dqa[part, :] + dqr[part, :].astype(F32)).astype(BF16)
        give(k, oq, dq_ref, 0)

    sent = pl.ds(0, HALF - ROWS)
    for a in range(4):
        took(qb.at[0, sent], s_in.at[a])
    took(drec.at[pl.ds(0, CHIPS - 1)], s_d)
    for a in range(2):
        took(qb.at[0], s_z.at[a])
        took(qb.at[0], s_c.at[a])
        took(rka, s_kv.at[a])
    tell.wait_send()
    took(st_oth, s_so)
    took(dqs, s_dz)
    for a, out in enumerate((dq_ref, dk_ref, dv_ref)):
        took(out, r_out.at[a])
        took(qb.at[0, sent], s_out.at[a])


def place(dq, dk, dv, dq_out, dk_out, dv_out, sem):
    copies = [
        pltpu.make_async_copy(src, dst, sem.at[n])
        for n, (src, dst) in enumerate(((dq, dq_out), (dk, dk_out), (dv, dv_out)))
    ]
    for copy in copies:
        copy.start()
    for copy in copies:
        copy.wait()


def body(queries, keys, values, outputs, d_outputs, tile_mask, tile_order):
    half = (HALF, DH)
    dma = pltpu.SemaphoreType.DMA
    hbm = pl.BlockSpec(memory_space=pl.ANY)
    grads = pl.pallas_call(
        kernel,
        out_shape=[jax.ShapeDtypeStruct(queries.shape, BF16)] * 3,
        in_specs=[hbm] * 7,
        out_specs=[hbm] * 3,
        scratch_shapes=[
            pltpu.VMEM((2,) + half, BF16),
            pltpu.VMEM((2 * HALF, DH), BF16),
            pltpu.VMEM((2 * HALF, DH), BF16),
            pltpu.VMEM((2,) + half, BF16),
            pltpu.VMEM((2, 4, 2 * HALF, GROUP), F32),
            pltpu.VMEM((2 * HALF, DH), F32),
            pltpu.VMEM((2 * HALF, DH), F32),
            pltpu.VMEM(half, F32),
            pltpu.VMEM(half, F32),
            pltpu.VMEM(half, F32),
            pltpu.VMEM(half, BF16),
            pltpu.VMEM(half, BF16),
            pltpu.VMEM(half, BF16),
            pltpu.VMEM(half, BF16),
            pltpu.VMEM(half, BF16),
            pltpu.VMEM(outputs.shape, BF16),
            pltpu.VMEM(outputs.shape, BF16),
            pltpu.SMEM(tile_mask.shape, jnp.int32),
            pltpu.SMEM(tile_order.shape, jnp.int32),
            pltpu.VMEM((BLOCK, BLOCK), F32),
            pltpu.VMEM((CHIPS, 1, BLOCK), F32),
            pltpu.VMEM((CHIPS, 1, BLOCK), F32),
            pltpu.VMEM((4, 3, 1, GROUP), F32),
            pltpu.VMEM((4, 2, 1, GROUP), F32),
            pltpu.VMEM((4, 3, 1, GROUP), F32),
            pltpu.VMEM((4, 2, 1, GROUP), F32),
            pltpu.VMEM((2, 16, 1, HALF), F32),
            dma((4,)),
            dma((4,)), dma((4, 4)),
            dma((2,)), dma((2, 4)),
            dma((2,)), dma((2,)),
            dma, dma,
            dma, dma,
            dma, dma((4,)),
            dma, dma((4,)),
            dma((2,)), dma((2, 4)),
            dma((3,)), dma((3,)),
        ],
        compiler_params=pltpu.CompilerParams(
            collective_id=0, has_side_effects=True, vmem_limit_bytes=56 * 2**20
        ),
        cost_estimate=pl.CostEstimate(flops=5 * 2**30, bytes_accessed=2**21, transcendentals=2**22),
        name="attention_backward",
    )(queries, keys, values, outputs, d_outputs, tile_mask, tile_order)
    return pl.pallas_call(
        place,
        out_shape=[jax.ShapeDtypeStruct(queries.shape, BF16)] * 3,
        in_specs=[pl.BlockSpec(memory_space=pltpu.VMEM)] * 3,
        out_specs=[hbm] * 3,
        scratch_shapes=[dma((3,))],
        name="place",
    )(*grads)


def solution(mesh):
    split = P(("dp", "blk", "head"), None)
    return jax.shard_map(
        body,
        mesh=mesh,
        in_specs=(split,) * 5 + (P(), P()),
        out_specs=(split,) * 3,
        check_vma=False,
    )
```

time: 98.6 us -> 62.9 us (0.64)
  the two profiles are of different devices: /device:TPU:1 before, /device:TPU:33 now
where the time goes in v2:
time: 62.9 us; the launch traced here: 62.8 us
  Pallas kernels  62.2 us (99%)
  between operations  0.64 us (1%)
    pallas_call x1, Pallas kernels, body(): pl.pallas_call(kernel, out_shape=[jax.ShapeDtypeStruct(queries.shape, BF1...  60.2 us
    pallas_call x1, Pallas kernels, body(): pl.pallas_call(place, out_shape=[jax.ShapeDtypeStruct(queries.shape, BF16...  2.01 us

profile of v2, /device:TPU:33, one launch (start us, length us, event | category | flops | bytes accessed | tf_op | source)
XLA Modules:
  0.0 62.8 jit_solution(4771836811880203514)
XLA Ops:
  0.6 60.2 %attention_backward.1 = (bf16[64,2048]{1,0:T(8,128)(2,1)}, bf16[64,2048]{1,0:T(8,128)(2,1)}, bf16[64,2048]{1,0:T(8,128)(2,1)}) custom-call(bf16[64,2048]{1,0:T(8,128)(2,1)} %q_ref.1, bf16[64,2048]{1,0:T(8,128)(2,1)} %k_ref.1, bf16[64,2048]{1,0:T(8,128)(2,1)} %v_ref.1, bf16[64,2048]{1,0:T(8,128)(2,1)} %o_ref.1, bf16[64,2048]{1,0:T(8,128)(2,1)} %g_ref.1, ...), custom_call_target="tpu_custom_call" | custom-call | flops 5368709120 | bytes 2097152 | tf_op jit(solution)/shard_map/attention_backward/pallas_call | solution.py:308
  60.8 2.0 %place.1 = (bf16[64,2048]{1,0:T(8,128)(2,1)}, bf16[64,2048]{1,0:T(8,128)(2,1)}, bf16[64,2048]{1,0:T(8,128)(2,1)}) custom-call(bf16[64,2048]{1,0:T(8,128)(2,1)} %get-tuple-element.6.dq, bf16[64,2048]{1,0:T(8,128)(2,1)} %get-tuple-element.7.dk, bf16[64,2048]{1,0:T(8,128)(2,1)} %get-tuple-element.8.dv), custom_call_target="tpu_custom_call" | custom-call | tf_op jit(solution)/shard_map/place/pallas_call | solution.py:358

commit v3 on v2

--- a/solution.py
+++ b/solution.py
@@ -103,7 +103,7 @@
 
     def forward_z(a, buf, first, last):
         def one(k, carry):
-            yy = group(k)
+            yy = group((k + a) % 4)
             part = rows(yy * GROUP, GROUP)
             took(buf.at[0, part], r_in.at[2 * a, yy])
             remote(buf.at[0, part], buf.at[1, part], s_z.at[a], r_z.at[a, yy], across).start()
@@ -211,7 +211,7 @@
         return carry
 
     def other(k, carry):
-        yy = group(k)
+        yy = group((k + 1) % 4)
         part = rows(yy * GROUP, GROUP)
         took(gb.at[1, part], r_z.at[1, yy])
         dqs[part, :] = gradients(1, yy, st_oth, pr_own, pr_own[yy, 2]).astype(BF16)
@@ -219,19 +219,19 @@
         return carry
 
     forward_core(0, kb)
-    forward_z(1, gb, 0, 1)
     took(kb.at[pl.ds((1 - c) * HALF, HALF)], r_c.at[0])
-    lax.fori_loop(0, 3, weigh_other, 0)
-    forward_z(1, gb, 1, 2)
-    forward_core(1, vb)
     lax.fori_loop(0, 4, weigh_own, 0)
     took(drec, r_d)
     for j in range(8):
         st_own[j // 2, 2, :, j % 2 * BLOCK : (j % 2 + 1) * BLOCK] = drec[2 * j] + drec[2 * j + 1]
     tell = remote(st_own, pr_own, s_st, r_st, across)
     tell.start()
+    forward_z(1, gb, 0, 1)
+    lax.fori_loop(0, 3, weigh_other, 0)
+    forward_z(1, gb, 1, 3)
+    forward_core(1, vb)
     lax.fori_loop(3, 4, weigh_other, 0)
-    forward_z(1, gb, 2, 4)
+    forward_z(1, gb, 3, 4)
     took(vb.at[pl.ds((1 - c) * HALF, HALF)], r_c.at[1])
     lax.fori_loop(0, 3, own, 0)
     tell.wait_recv()
@@ -239,7 +239,7 @@
     lax.fori_loop(3, 4, own, 0)
     lax.fori_loop(2, 4, other, 0)
 
-    for k in range(4):
+    for k in (1, 2, 3, 0):
         yy = group(k)
         part = rows(yy * GROUP, GROUP)
         there = rows((1 - c) * HALF + yy * GROUP, GROUP)
@@ -248,7 +248,7 @@
 
     def give(k, buf, out, a):
         yy = group(k)
-        for kx in range(4):
+        for kx in (2, 1, 3, 0):
             px = (x + kx) % 4
             piece = buf.at[rows((yy * 4 + px) * ROWS, ROWS)]
             home = out.at[:, rows(me * DH, DH)]
@@ -257,7 +257,7 @@
             else:
                 remote(piece, home, s_out.at[a], r_out.at[a], plane(px, yy)).start()
 
-    for k in range(4):
+    for k in (1, 2, 3, 0):
         yy = group(k)
         part = rows(yy * GROUP, GROUP)
         here = rows(c * HALF + yy * GROUP, GROUP)
@@ -267,7 +267,7 @@
         took(rka.at[part], r_kv.at[0, yy])
         ok[part, :] = (dka[here, :] + rka[part, :]).astype(BF16)
         give(k, ok, dk_ref, 1)
-    for k in range(4):
+    for k in (1, 2, 3, 0):
         yy = group(k)
         part = rows(yy * GROUP, GROUP)
         took(dqr.at[part], r_dz.at[yy])

time: 62.9 us -> 59.7 us (0.949)
  the two profiles are of different devices: /device:TPU:33 before, /device:TPU:1 now
where the time goes in v3:
time: 59.7 us; the launch traced here: 59.6 us
  Pallas kernels  59 us (99%)
  between operations  0.64 us (1%)
    pallas_call x1, Pallas kernels, body(): pl.pallas_call(kernel, out_shape=[jax.ShapeDtypeStruct(queries.shape, BF1...  57 us
    pallas_call x1, Pallas kernels, body(): pl.pallas_call(place, out_shape=[jax.ShapeDtypeStruct(queries.shape, BF16...  2.01 us

profile of v3, /device:TPU:1, one launch (start us, length us, event | category | flops | bytes accessed | tf_op | source)
XLA Modules:
  0.0 59.6 jit_solution(14027296579400529604)
XLA Ops:
  0.6 57.0 %attention_backward.1 = (bf16[64,2048]{1,0:T(8,128)(2,1)}, bf16[64,2048]{1,0:T(8,128)(2,1)}, bf16[64,2048]{1,0:T(8,128)(2,1)}) custom-call(bf16[64,2048]{1,0:T(8,128)(2,1)} %q_ref.1, bf16[64,2048]{1,0:T(8,128)(2,1)} %k_ref.1, bf16[64,2048]{1,0:T(8,128)(2,1)} %v_ref.1, bf16[64,2048]{1,0:T(8,128)(2,1)} %o_ref.1, bf16[64,2048]{1,0:T(8,128)(2,1)} %g_ref.1, ...), custom_call_target="tpu_custom_call" | custom-call | flops 5368709120 | bytes 2097152 | tf_op jit(solution)/shard_map/attention_backward/pallas_call | solution.py:308
  57.6 2.0 %place.1 = (bf16[64,2048]{1,0:T(8,128)(2,1)}, bf16[64,2048]{1,0:T(8,128)(2,1)}, bf16[64,2048]{1,0:T(8,128)(2,1)}) custom-call(bf16[64,2048]{1,0:T(8,128)(2,1)} %get-tuple-element.6.dq, bf16[64,2048]{1,0:T(8,128)(2,1)} %get-tuple-element.7.dk, bf16[64,2048]{1,0:T(8,128)(2,1)} %get-tuple-element.8.dv), custom_call_target="tpu_custom_call" | custom-call | tf_op jit(solution)/shard_map/place/pallas_call | solution.py:358

commit v4 on v3

--- a/solution.py
+++ b/solution.py
@@ -179,7 +179,7 @@
         stats[yy, 0] = top
         stats[yy, 1] = jnp.sum(total, axis=0, keepdims=True)
 
-    def gradients(half, yy, stats, theirs, delta):
+    def gradients(half, yy, stats, theirs, delta, keys=slice(None)):
         lanes = rows(yy * GROUP, GROUP)
         query = qb[half, lanes, :]
         dout = gb[half, lanes, :]
@@ -187,11 +187,11 @@
         high = jnp.maximum(top, top_r)
         ours = jnp.exp2(top - high)
         factor = ours / (total * ours + total_r * jnp.exp2(top_r - high))
-        e = ee[half, yy]
-        ds = (e * (factor * SCALE) * (mm(vb[...], dout, NT) - delta)).astype(BF16)
-        dva[...] += mm((e * factor).astype(BF16), dout, NN)
-        dka[...] += mm(ds, query, NN)
-        return mm(ds, kb[...], TN)
+        e = ee[half, yy, keys, :]
+        ds = (e * (factor * SCALE) * (mm(vb[keys, :], dout, NT) - delta)).astype(BF16)
+        dva[keys, :] += mm((e * factor).astype(BF16), dout, NN)
+        dka[keys, :] += mm(ds, query, NN)
+        return mm(ds, kb[keys, :], TN)
 
     def weigh_own(k, carry):
         weigh(0, group(k), st_own)
@@ -237,14 +237,23 @@
     tell.wait_recv()
     lax.fori_loop(0, 2, other, 0)
     lax.fori_loop(3, 4, own, 0)
-    lax.fori_loop(2, 4, other, 0)
-
+    lax.fori_loop(2, 3, other, 0)
+
+    last = group(0)
+    part_last = rows(last * GROUP, GROUP)
+    took(gb.at[1, part_last], r_z.at[1, last])
+    theirs = rows((1 - c) * HALF, HALF)
+    dq_last = gradients(1, last, st_oth, pr_own, pr_own[last, 2], theirs)
     for k in (1, 2, 3, 0):
         yy = group(k)
         part = rows(yy * GROUP, GROUP)
         there = rows((1 - c) * HALF + yy * GROUP, GROUP)
         remote(dva.at[there], rva.at[part], s_kv.at[1], r_kv.at[1, yy], sibling).start()
         remote(dka.at[there], rka.at[part], s_kv.at[0], r_kv.at[0, yy], sibling).start()
+    dq_last += gradients(1, last, st_oth, pr_own, pr_own[last, 2], rows(c * HALF, HALF))
+    dqs[part_last, :] = dq_last.astype(BF16)
+    remote(dqs.at[part_last], dqr.at[part_last], s_dz, r_dz.at[last], across).start()
+
 
     def give(k, buf, out, a):
         yy = group(k)

time: 59.7 us -> 60.1 us (level)
  no operation moved by 1% of the time
where the time goes in v4:
time: 60.1 us; the launch traced here: 59.9 us
  Pallas kernels  59.3 us (99%)
  between operations  0.64 us (1%)
    pallas_call x1, Pallas kernels, body(): pl.pallas_call(kernel, out_shape=[jax.ShapeDtypeStruct(queries.shape, BF1...  57.3 us
    pallas_call x1, Pallas kernels, body(): pl.pallas_call(place, out_shape=[jax.ShapeDtypeStruct(queries.shape, BF16...  2.01 us

profile of v4, /device:TPU:1, one launch (start us, length us, event | category | flops | bytes accessed | tf_op | source)
XLA Modules:
  0.0 59.9 jit_solution(3313537732851883865)
XLA Ops:
  0.6 57.3 %attention_backward.1 = (bf16[64,2048]{1,0:T(8,128)(2,1)}, bf16[64,2048]{1,0:T(8,128)(2,1)}, bf16[64,2048]{1,0:T(8,128)(2,1)}) custom-call(bf16[64,2048]{1,0:T(8,128)(2,1)} %q_ref.1, bf16[64,2048]{1,0:T(8,128)(2,1)} %k_ref.1, bf16[64,2048]{1,0:T(8,128)(2,1)} %v_ref.1, bf16[64,2048]{1,0:T(8,128)(2,1)} %o_ref.1, bf16[64,2048]{1,0:T(8,128)(2,1)} %g_ref.1, ...), custom_call_target="tpu_custom_call" | custom-call | flops 5368709120 | bytes 2097152 | tf_op jit(solution)/shard_map/attention_backward/pallas_call | solution.py:317
  57.9 2.0 %place.1 = (bf16[64,2048]{1,0:T(8,128)(2,1)}, bf16[64,2048]{1,0:T(8,128)(2,1)}, bf16[64,2048]{1,0:T(8,128)(2,1)}) custom-call(bf16[64,2048]{1,0:T(8,128)(2,1)} %get-tuple-element.6.dq, bf16[64,2048]{1,0:T(8,128)(2,1)} %get-tuple-element.7.dk, bf16[64,2048]{1,0:T(8,128)(2,1)} %get-tuple-element.8.dv), custom_call_target="tpu_custom_call" | custom-call | tf_op jit(solution)/shard_map/place/pallas_call | solution.py:367
